TPU v7x, 512 devices: a whole 4x4x16 slice. The times are simulated.
512 devices in a mesh: dp: 32 (over y, x, core), mem: 16 (over z).
Axes of the slice: x: 4, y: 4, z: 16, core: 2. Of those that a mesh axis runs over, the one named last changes fastest.
Arguments:
- queries: bfloat16 [32, 2048, 2048], P('dp', 'mem'), may hold values from -6 to 6
- seg_keys: bfloat16 [32, 2048, 2048], P('dp', 'mem'), may hold values from -6 to 6
- seg_values: bfloat16 [32, 2048, 2048], P('dp', 'mem'), may hold values from -6 to 6
- mem_keys: bfloat16 [32, 2, 16, 128, 2048], P('dp', None, 'mem'), may hold values from -6 to 6
- mem_values: bfloat16 [32, 2, 16, 128, 2048], P('dp', None, 'mem'), may hold values from -6 to 6
- block_ids: int32 [32, 16, 16, 16], P('dp', None, 'mem'), may hold values from 0 to 31, as said below
- pointer: int32 [32], P('dp'), may hold values from 0 to 16, as said below
- gate_bias: float32 [16], P('mem'), may hold values from -2 to 2
- out_weight: bfloat16 [2048, 2048], P('dp'), may hold values from -0.125 to 0.125
Outputs:
- layer_out: bfloat16 [32, 2048, 2048], P('dp', 'mem')
Inputs may be any that keep to these rules, and one draw needn't show every extreme that they name: `pointer`: a multiple of 16. `block_ids`: for each query block and head 16 distinct slots; query block i never names slot pointer + j with j >= i.
All inputs are finite; a program needn't handle non-finite values.
Results may differ from a plain program's by a relative error of at most 0.0056.
Values may be sent and summed in bfloat16 or wider, within the bound.
A program may use at most 64 MiB of HBM per device.

v0:
```python
import math

import jax
import jax.numpy as jnp
from jax import lax
from jax.sharding import PartitionSpec as P

HD = 128
BLK = 128


def softmax_rows(scores):
    highest = jnp.max(scores, axis=-1, keepdims=True)
    expo = jnp.exp(scores - highest)
    return expo / jnp.sum(expo, axis=-1, keepdims=True)


def causal_attention(query_h, key_h, value_h):
    score_scale = 1.0 / math.sqrt(HD)
    length = query_h.shape[0]
    block_rows = min(512, length)
    pieces = []
    for block in range(length // block_rows):
        finish = (block + 1) * block_rows
        scores = (
            jnp.einsum(
                "qd,kd->qk",
                query_h[block * block_rows : finish],
                key_h[:finish],
                preferred_element_type=jnp.float32,
            )
            * score_scale
        )
        row_index = block * block_rows + jnp.arange(block_rows)
        causal_mask = row_index[:, None] >= jnp.arange(finish)[None, :]
        scores = jnp.where(causal_mask, scores, -1e30)
        weights = softmax_rows(scores).astype(jnp.bfloat16)
        pieces.append(jnp.dot(weights, value_h[:finish], preferred_element_type=jnp.float32))
    return jnp.concatenate(pieces, axis=0)


def memory_attention(query_h, memk_h, memv_h, positions):
    score_scale = 1.0 / math.sqrt(HD)
    block_count = positions.shape[0]
    group = min(4, block_count)
    query_groups = query_h.reshape(block_count // group, group, BLK, HD)
    slot_groups = positions.reshape(block_count // group, group, positions.shape[1])

    def one_group(inputs):
        query_part, slot_part = inputs
        fetched_k = memk_h[slot_part].reshape(group, -1, HD)
        fetched_v = memv_h[slot_part].reshape(group, -1, HD)
        scores = (
            jnp.einsum("gtd,gkd->gtk", query_part, fetched_k, preferred_element_type=jnp.float32)
            * score_scale
        )
        weights = softmax_rows(scores).astype(jnp.bfloat16)
        return jnp.einsum("gtk,gkd->gtd", weights, fetched_v, preferred_element_type=jnp.float32)

    return lax.map(one_group, (query_groups, slot_groups)).reshape(-1, HD)


def local(
    queries, seg_keys, seg_values, mem_keys, mem_values, block_ids, pointer, gate_bias, out_weight
):
    owners = lax.axis_size("mem")
    model_width = queries.shape[2]
    query_all, key_all, value_all = (
        lax.all_to_all(queries[0], "mem", split_axis=1, concat_axis=0, tiled=True),
        lax.all_to_all(seg_keys[0], "mem", split_axis=1, concat_axis=0, tiled=True),
        lax.all_to_all(seg_values[0], "mem", split_axis=1, concat_axis=0, tiled=True),
    )
    feature_width = query_all.shape[1]
    slots_here = mem_keys.shape[1]
    memk_all, memv_all = (
        lax.all_to_all(
            mem_keys[0, :, 0].reshape(slots_here * BLK, model_width),
            "mem",
            split_axis=1,
            concat_axis=0,
            tiled=True,
        ),
        lax.all_to_all(
            mem_values[0, :, 0].reshape(slots_here * BLK, model_width),
            "mem",
            split_axis=1,
            concat_axis=0,
            tiled=True,
        ),
    )
    memk_all = memk_all.reshape(owners, slots_here, BLK, feature_width)
    memv_all = memv_all.reshape(owners, slots_here, BLK, feature_width)
    column_slot = pointer[0] // owners
    zero_index = jnp.zeros((), jnp.int32)
    update_at = (zero_index, column_slot, zero_index, zero_index)
    memk_all = lax.dynamic_update_slice(
        memk_all, key_all.reshape(owners, 1, BLK, feature_width), update_at
    )
    memv_all = lax.dynamic_update_slice(
        memv_all, value_all.reshape(owners, 1, BLK, feature_width), update_at
    )
    memk_flat = memk_all.reshape(owners * slots_here, BLK, feature_width)
    memv_flat = memv_all.reshape(owners * slots_here, BLK, feature_width)
    positions = block_ids[0] % owners * slots_here + block_ids[0] // owners
    gates = jax.nn.sigmoid(gate_bias)
    local_out = causal_attention(query_all, key_all, value_all)
    memory_out = memory_attention(query_all, memk_flat, memv_flat, positions[:, 0, :])
    mixed = gates[0] * memory_out + (1.0 - gates[0]) * local_out
    attended_heads = mixed.astype(jnp.bfloat16)
    token_feats = lax.all_to_all(attended_heads, "mem", split_axis=0, concat_axis=1, tiled=True)
    projected = jnp.dot(
        token_feats,
        lax.all_gather(out_weight, "dp", axis=0, tiled=True),
        preferred_element_type=jnp.float32,
    )
    result = projected.astype(jnp.bfloat16)
    return result[None]


def solution(mesh):
    in_specs = (
        P("dp", "mem", None),
        P("dp", "mem", None),
        P("dp", "mem", None),
        P("dp", None, "mem", None, None),
        P("dp", None, "mem", None, None),
        P("dp", None, "mem", None),
        P("dp"),
        P("mem"),
        P("dp", None),
    )
    out_specs = P("dp", "mem", None)
    return jax.shard_map(local, mesh=mesh, in_specs=in_specs, out_specs=out_specs, check_vma=False)
```

profile of v0, /device:TPU:1, one launch (start us, length us, event | category | flops | bytes accessed | tf_op | source)
XLA Modules:
  0.0 339.6 jit_solution(5149211862903952358)
XLA Ops:
  6.5 1.2 copy.34
  7.8 0.9 copy.27
  8.7 15.7 %all-to-all-start = ((bf16[128,16,128]{2,0,1:T(8,128)(2,1)}), bf16[128,16,128]{2,0,1:T(8,128)(2,1)S(1)}, u32[]{:S(2)}, u32[]{:S(2)}) async-start(bf16[128,16,128]{2,0,1:T(8,128)(2,1)} %copy.27), calls=%async_computation | async-start | bytes 1048576 | tf_op jit(solution)/shard_map/all_to_all | solution.py:69
  24.6 0.9 copy.29
  25.5 21.8 %all-to-all-done = bf16[128,16,128]{2,0,1:T(8,128)(2,1)S(1)} async-done(((bf16[128,16,128]{2,0,1:T(8,128)(2,1)}), bf16[128,16,128]{2,0,1:T(8,128)(2,1)S(1)}, u32[]{:S(2)}, u32[]{:S(2)}) %all-to-all-start) | async-done | bytes 524320 | tf_op jit(solution)/shard_map/all_to_all | solution.py:69
  47.3 12.6 %all-to-all-start.2 = ((bf16[128,16,128]{2,0,1:T(8,128)(2,1)}), bf16[128,16,128]{2,0,1:T(8,128)(2,1)S(1)}, u32[]{:S(2)}, u32[]{:S(2)}) async-start(bf16[128,16,128]{2,0,1:T(8,128)(2,1)} %copy.29), calls=%async_computation.2 | async-start | bytes 1048576 | tf_op jit(solution)/shard_map/all_to_all | solution.py:70
  60.0 0.9 copy.31
  61.0 21.7 %all-to-all-done.2 = bf16[128,16,128]{2,0,1:T(8,128)(2,1)S(1)} async-done(((bf16[128,16,128]{2,0,1:T(8,128)(2,1)}), bf16[128,16,128]{2,0,1:T(8,128)(2,1)S(1)}, u32[]{:S(2)}, u32[]{:S(2)}) %all-to-all-start.2) | async-done | bytes 524320 | tf_op jit(solution)/shard_map/all_to_all | solution.py:70
  82.7 12.6 %all-to-all-start.4 = ((bf16[128,16,128]{2,0,1:T(8,128)(2,1)}), bf16[128,16,128]{2,0,1:T(8,128)(2,1)S(1)}, u32[]{:S(2)}, u32[]{:S(2)}) async-start(bf16[128,16,128]{2,0,1:T(8,128)(2,1)} %copy.31), calls=%async_computation.4 | async-start | bytes 1048576 | tf_op jit(solution)/shard_map/all_to_all | solution.py:71
  96.1 1.5 copy.35
  97.5 1.3 copy.28
  98.8 19.3 %all-to-all-done.4 = bf16[128,16,128]{2,0,1:T(8,128)(2,1)S(1)} async-done(((bf16[128,16,128]{2,0,1:T(8,128)(2,1)}), bf16[128,16,128]{2,0,1:T(8,128)(2,1)S(1)}, u32[]{:S(2)}, u32[]{:S(2)}) %all-to-all-start.4) | async-done | bytes 524320 | tf_op jit(solution)/shard_map/all_to_all | solution.py:71
  118.1 12.7 %all-to-all-start.1 = ((bf16[256,16,128]{2,0,1:T(8,128)(2,1)}), bf16[256,16,128]{2,0,1:T(8,128)(2,1)S(1)}, u32[]{:S(2)}, u32[]{:S(2)}) async-start(bf16[256,16,128]{2,0,1:T(8,128)(2,1)} %copy.28), calls=%async_computation.1 | async-start | bytes 2097152 | tf_op jit(solution)/shard_map/all_to_all | solution.py:76
  132.2 1.5 copy.37
  133.7 1.2 copy.30
  138.5 1.3 fusion.44
  139.8 2.4 fusion.43
  142.3 33.5 %all-to-all-done.1 = bf16[256,16,128]{2,0,1:T(8,128)(2,1)S(1)} async-done(((bf16[256,16,128]{2,0,1:T(8,128)(2,1)}), bf16[256,16,128]{2,0,1:T(8,128)(2,1)S(1)}, u32[]{:S(2)}, u32[]{:S(2)}) %all-to-all-start.1) | async-done | bytes 1048608 | tf_op jit(solution)/shard_map/all_to_all | solution.py:76
  175.8 13.0 %all-to-all-start.3 = ((bf16[256,16,128]{2,0,1:T(8,128)(2,1)}), bf16[256,16,128]{2,0,1:T(8,128)(2,1)S(1)}, u32[]{:S(2)}, u32[]{:S(2)}) async-start(bf16[256,16,128]{2,0,1:T(8,128)(2,1)} %copy.30), calls=%async_computation.3 | async-start | bytes 2097152 | tf_op jit(solution)/shard_map/all_to_all | solution.py:83
  188.9 1.5 fusion.31
  190.3 2.0 fusion.26
  192.4 1.5 fusion.42
  194.9 1.0 fusion.41
  199.6 1.1 maximum_multiply_fusion
  200.7 2.6 copy.33
  203.4 30.7 %all-to-all-done.3 = bf16[256,16,128]{2,0,1:T(8,128)(2,1)S(1)} async-done(((bf16[256,16,128]{2,0,1:T(8,128)(2,1)}), bf16[256,16,128]{2,0,1:T(8,128)(2,1)S(1)}, u32[]{:S(2)}, u32[]{:S(2)}) %all-to-all-start.3) | async-done | bytes 1048608 | tf_op jit(solution)/shard_map/all_to_all | solution.py:83
  234.1 55.8 %while.10 = (s32[]{:T(128)}, f32[4,4,128,128]{3,2,1,0:T(8,128)}, bf16[4,4,128,128]{3,2,1,0:T(8,128)(2,1)}, s32[4,4,16]{2,1,0:T(4,128)S(1)}, bf16[32,128,128]{2,1...) while((s32[]{:T(128)}, f32[4,4,128,128]{3,2,1,0:T(8,128)}, ...), condition=%wide.region_3.4_spmd, body=%wide.region_0.3_spmd.sunk | while | flops 542117056 | bytes 29764488 | solution.py:60
  235.1 0.9 gather_fusion.1
  236.1 4.2 %fusion.69 = (f32[4,128]{1,0:T(4,128)S(1)}, f32[4,128,2048]{2,1,0:T(8,128)}) fusion(bf16[4,2048,128]{2,1,0:T(8,128)(2,1)S(1)} %bitcast.117, bf16[4,4,128,128]{3,2,1,0:T(8,128)(2,1)} %get-tuple-element.121, s32[]{:T(128)} %get-tuple-element.112), kind=kOutput, calls=%fused_computation.69.clone.1 | convolution fusion | flops 271583232 | bytes 6425088 | tf_op jit(solution)/shard_map/while/body/eval_jaxpr/sub | solution.py:14
  240.3 3.4 gather_fusion
  243.7 4.4 %fusion.70 = f32[4,4,128,128]{3,2,1,0:T(8,128)} fusion(f32[4,4,128,128]{3,2,1,0:T(8,128)} %get-tuple-element.113, s32[]{:T(128)} %get-tuple-element.112, bf16[4,2048,128]{2,1,0:T(8,128)(2,1)} %bitcast.122, f32[4,128,2048]{2,1,0:T(8,128)} %get-tuple-element.103, f32[4,128]{1,0:T(4,128)S(1)} %get-tuple-element.104), kind=kOutput, calls=%fused_computation.10.clone.1 | convolution fusion | flops 270532608 | bytes 6556160 | tf_op jit(solution)/shard_map/while/body/eval_jaxpr/gtk,gkd->gtd/dot_general | solution.py:58
  248.2 0.9 copy-done
  249.1 0.9 gather_fusion.1
  250.0 4.2 %fusion.69 = (f32[4,128]{1,0:T(4,128)S(1)}, f32[4,128,2048]{2,1,0:T(8,128)}) fusion(bf16[4,2048,128]{2,1,0:T(8,128)(2,1)S(1)} %bitcast.117, bf16[4,4,128,128]{3,2,1,0:T(8,128)(2,1)} %get-tuple-element.121, s32[]{:T(128)} %get-tuple-element.112), kind=kOutput, calls=%fused_computation.69.clone.1 | convolution fusion | flops 271583232 | bytes 6425088 | tf_op jit(solution)/shard_map/while/body/eval_jaxpr/sub | solution.py:14
  254.3 3.4 gather_fusion
  257.6 4.4 %fusion.70 = f32[4,4,128,128]{3,2,1,0:T(8,128)} fusion(f32[4,4,128,128]{3,2,1,0:T(8,128)} %get-tuple-element.113, s32[]{:T(128)} %get-tuple-element.112, bf16[4,2048,128]{2,1,0:T(8,128)(2,1)} %bitcast.122, f32[4,128,2048]{2,1,0:T(8,128)} %get-tuple-element.103, f32[4,128]{1,0:T(4,128)S(1)} %get-tuple-element.104), kind=kOutput, calls=%fused_computation.10.clone.1 | convolution fusion | flops 270532608 | bytes 6556160 | tf_op jit(solution)/shard_map/while/body/eval_jaxpr/gtk,gkd->gtd/dot_general | solution.py:58
  262.1 0.9 copy-done
  263.0 0.9 gather_fusion.1
  264.0 4.2 %fusion.69 = (f32[4,128]{1,0:T(4,128)S(1)}, f32[4,128,2048]{2,1,0:T(8,128)}) fusion(bf16[4,2048,128]{2,1,0:T(8,128)(2,1)S(1)} %bitcast.117, bf16[4,4,128,128]{3,2,1,0:T(8,128)(2,1)} %get-tuple-element.121, s32[]{:T(128)} %get-tuple-element.112), kind=kOutput, calls=%fused_computation.69.clone.1 | convolution fusion | flops 271583232 | bytes 6425088 | tf_op jit(solution)/shard_map/while/body/eval_jaxpr/sub | solution.py:14
  268.2 3.4 gather_fusion
  271.6 4.4 %fusion.70 = f32[4,4,128,128]{3,2,1,0:T(8,128)} fusion(f32[4,4,128,128]{3,2,1,0:T(8,128)} %get-tuple-element.113, s32[]{:T(128)} %get-tuple-element.112, bf16[4,2048,128]{2,1,0:T(8,128)(2,1)} %bitcast.122, f32[4,128,2048]{2,1,0:T(8,128)} %get-tuple-element.103, f32[4,128]{1,0:T(4,128)S(1)} %get-tuple-element.104), kind=kOutput, calls=%fused_computation.10.clone.1 | convolution fusion | flops 270532608 | bytes 6556160 | tf_op jit(solution)/shard_map/while/body/eval_jaxpr/gtk,gkd->gtd/dot_general | solution.py:58
  277.0 0.9 gather_fusion.1
  277.9 4.2 %fusion.69 = (f32[4,128]{1,0:T(4,128)S(1)}, f32[4,128,2048]{2,1,0:T(8,128)}) fusion(bf16[4,2048,128]{2,1,0:T(8,128)(2,1)S(1)} %bitcast.117, bf16[4,4,128,128]{3,2,1,0:T(8,128)(2,1)} %get-tuple-element.121, s32[]{:T(128)} %get-tuple-element.112), kind=kOutput, calls=%fused_computation.69.clone.1 | convolution fusion | flops 271583232 | bytes 6425088 | tf_op jit(solution)/shard_map/while/body/eval_jaxpr/sub | solution.py:14
  282.2 3.4 gather_fusion
  285.5 4.4 %fusion.70 = f32[4,4,128,128]{3,2,1,0:T(8,128)} fusion(f32[4,4,128,128]{3,2,1,0:T(8,128)} %get-tuple-element.113, s32[]{:T(128)} %get-tuple-element.112, bf16[4,2048,128]{2,1,0:T(8,128)(2,1)} %bitcast.122, f32[4,128,2048]{2,1,0:T(8,128)} %get-tuple-element.103, f32[4,128]{1,0:T(4,128)S(1)} %get-tuple-element.104), kind=kOutput, calls=%fused_computation.10.clone.1 | convolution fusion | flops 270532608 | bytes 6556160 | tf_op jit(solution)/shard_map/while/body/eval_jaxpr/gtk,gkd->gtd/dot_general | solution.py:58
  290.0 1.4 broadcast_multiply_fusion
  291.9 35.4 %all_to_all.102 = bf16[16,128,128]{1,2,0:T(8,128)(2,1)S(1)} all-to-all(bf16[16,128,128]{1,2,0:T(8,128)(2,1)S(1)} %fusion.29), channel_id=1, replica_groups=mesh['dp'=32,'mem'=16] {'mem'}, dimensions={0} | all-to-all | bytes 1048576 | tf_op jit(solution)/shard_map/all_to_all | solution.py:110
  327.3 5.5 %fusion.24 = bf16[1,128,2048]{2,1,0:T(8,128)(2,1)} fusion(bf16[128,2048]{0,1:T(8,128)(2,1)S(1)} %bitcast.133, bf16[2048,2048]{1,0:T(8,128)(2,1)} %all-gather.2.cloned.1.call-done), kind=kOutput, calls=%fused_computation.34 | convolution fusion | flops 1074003968 | bytes 9437184 | tf_op jit(solution)/shard_map/dot_general | solution.py:111
  (79 shorter events, 11.9 us)
Async XLA Ops:
  6.5 17.9 %copy-start.6 = (bf16[1,128,2048]{2,1,0:T(8,128)(2,1)S(1)}, bf16[1,128,2048]{2,1,0:T(8,128)(2,1)}, u32[]{:S(2)}) copy-start(bf16[1,128,2048]{2,1,0:T(8,128)(2,1)} %param.12) | copy-start | bytes 1572868
  6.5 53.3 %copy-start.7 = (bf16[1,128,2048]{2,1,0:T(8,128)(2,1)S(1)}, bf16[1,128,2048]{2,1,0:T(8,128)(2,1)}, u32[]{:S(2)}) copy-start(bf16[1,128,2048]{2,1,0:T(8,128)(2,1)} %param.13) | copy-start | bytes 1572868
  8.7 38.6 %all-to-all-start = ((bf16[128,16,128]{2,0,1:T(8,128)(2,1)}), bf16[128,16,128]{2,0,1:T(8,128)(2,1)S(1)}, u32[]{:S(2)}, u32[]{:S(2)}) async-start(bf16[128,16,128]{2,0,1:T(8,128)(2,1)} %copy.27), calls=%async_computation | async-start | bytes 1048576 | tf_op jit(solution)/shard_map/all_to_all | solution.py:69
  47.3 90.5 %copy-start.2 = (bf16[128,16,128]{2,0,1:T(8,128)(2,1)}, bf16[128,16,128]{2,0,1:T(8,128)(2,1)S(1)}, u32[]{:S(2)}) copy-start(bf16[128,16,128]{2,0,1:T(8,128)(2,1)S(1)} %all-to-all-done) | copy-start | bytes 1572868
  47.3 35.4 %all-to-all-start.2 = ((bf16[128,16,128]{2,0,1:T(8,128)(2,1)}), bf16[128,16,128]{2,0,1:T(8,128)(2,1)S(1)}, u32[]{:S(2)}, u32[]{:S(2)}) async-start(bf16[128,16,128]{2,0,1:T(8,128)(2,1)} %copy.29), calls=%async_computation.2 | async-start | bytes 1048576 | tf_op jit(solution)/shard_map/all_to_all | solution.py:70
  82.7 35.4 %all-to-all-start.4 = ((bf16[128,16,128]{2,0,1:T(8,128)(2,1)}), bf16[128,16,128]{2,0,1:T(8,128)(2,1)S(1)}, u32[]{:S(2)}, u32[]{:S(2)}) async-start(bf16[128,16,128]{2,0,1:T(8,128)(2,1)} %copy.31), calls=%async_computation.4 | async-start | bytes 1048576 | tf_op jit(solution)/shard_map/all_to_all | solution.py:71
  95.3 232.0 %all-gather.2.cloned.1.call-start = ((), (), s32[]{:S(2)}) async-start(), calls=%async_computation.6 | async-start | bytes 8650752 | tf_op jit(solution)/shard_map/all_gather | solution.py:113
  98.8 36.7 %copy-start.13 = (s32[1,16,1,16]{3,2,1,0:T(1,128)S(1)}, s32[1,16,1,16]{3,2,1,0:T(1,128)}, u32[]{:S(2)}) copy-start(s32[1,16,1,16]{3,2,1,0:T(1,128)} %param.16) | copy-start | bytes 3076
  118.1 57.7 %all-to-all-start.1 = ((bf16[256,16,128]{2,0,1:T(8,128)(2,1)}), bf16[256,16,128]{2,0,1:T(8,128)(2,1)S(1)}, u32[]{:S(2)}, u32[]{:S(2)}) async-start(bf16[256,16,128]{2,0,1:T(8,128)(2,1)} %copy.28), calls=%async_computation.1 | async-start | bytes 2097152 | tf_op jit(solution)/shard_map/all_to_all | solution.py:76
  175.8 58.3 %all-to-all-start.3 = ((bf16[256,16,128]{2,0,1:T(8,128)(2,1)}), bf16[256,16,128]{2,0,1:T(8,128)(2,1)S(1)}, u32[]{:S(2)}, u32[]{:S(2)}) async-start(bf16[256,16,128]{2,0,1:T(8,128)(2,1)} %copy.30), calls=%async_computation.3 | async-start | bytes 2097152 | tf_op jit(solution)/shard_map/all_to_all | solution.py:83
  188.8 3.5 %copy-start.8 = (bf16[12,128,128]{2,1,0:T(8,128)(2,1)S(1)}, bf16[12,128,128]{2,1,0:T(8,128)(2,1)}, u32[]{:S(2)}) copy-start(bf16[12,128,128]{2,1,0:T(8,128)(2,1)} %slice.91) | copy-start | bytes 1179652
  188.8 3.5 %copy-start.12 = (bf16[4,128,128]{2,1,0:T(8,128)(2,1)S(1)}, bf16[4,128,128]{2,1,0:T(8,128)(2,1)}, u32[]{:S(2)}) copy-start(bf16[4,128,128]{2,1,0:T(8,128)(2,1)} %get-tuple-element.53) | copy-start | bytes 393220
  192.4 2.1 copy-start.5
  192.4 2.1 copy-start.10
  193.9 0.9 copy-start.11
  195.9 1.6 copy-start.4
  195.9 1.6 copy-start.9
  195.9 1.6 copy-start.14
  234.2 1.0 copy-start
  243.7 4.4 %copy-start.1 = (bf16[32,128,128]{2,1,0:T(8,128)(2,1)S(1)}, bf16[32,128,128]{2,1,0:T(8,128)(2,1)}, u32[]{:S(2)}) copy-start(bf16[32,128,128]{2,1,0:T(8,128)(2,1)} %copy-done) | copy-start | bytes 3145732 | tf_op jit(solution)/shard_map/while
  248.1 1.0 copy-start
  257.6 4.4 %copy-start.1 = (bf16[32,128,128]{2,1,0:T(8,128)(2,1)S(1)}, bf16[32,128,128]{2,1,0:T(8,128)(2,1)}, u32[]{:S(2)}) copy-start(bf16[32,128,128]{2,1,0:T(8,128)(2,1)} %copy-done) | copy-start | bytes 3145732 | tf_op jit(solution)/shard_map/while
  262.0 1.0 copy-start
  271.6 4.4 %copy-start.1 = (bf16[32,128,128]{2,1,0:T(8,128)(2,1)S(1)}, bf16[32,128,128]{2,1,0:T(8,128)(2,1)}, u32[]{:S(2)}) copy-start(bf16[32,128,128]{2,1,0:T(8,128)(2,1)} %copy-done) | copy-start | bytes 3145732 | tf_op jit(solution)/shard_map/while
  276.0 1.0 copy-start
  285.5 4.4 %copy-start.1 = (bf16[32,128,128]{2,1,0:T(8,128)(2,1)S(1)}, bf16[32,128,128]{2,1,0:T(8,128)(2,1)}, u32[]{:S(2)}) copy-start(bf16[32,128,128]{2,1,0:T(8,128)(2,1)} %copy-done) | copy-start | bytes 3145732 | tf_op jit(solution)/shard_map/while
  290.0 1.8 copy-start.3
Sparse Core Ops, SparseCore 0:
  99.3 70.1 all-gather.1
where the time goes:
time: 346 us; the launch traced here: 340 us
  waiting for transfers between devices  128 us (37%)
  starting transfers between devices  66.7 us (19%)
  matrix products  48.8 us (14%)
  local copies, waits for them, and re-layouts  37.7 us (11%)
  blocking collectives  35.4 us (10%)
  between operations  15.1 us (4%)
  other arithmetic  8.09 us (2%)
    all_to_all x1, blocking collectives, local(): lax.all_to_all(attended_heads, 'mem', split_axis=0, concat_axis=1, tiled=...  35.4 us
    all_to_all x1, waiting for transfers between devices, local(): lax.all_to_all(mem_keys[0, :, 0].reshape(slots_here * BLK, model_width),...  33.5 us
    all_to_all x1, waiting for transfers between devices, local(): lax.all_to_all(mem_values[0, :, 0].reshape(slots_here * BLK, model_width)...  30.7 us
    all_to_all x1, waiting for transfers between devices, local(): lax.all_to_all(queries[0], 'mem', split_axis=1, concat_axis=0, tiled=True)  21.8 us
    all_to_all x1, waiting for transfers between devices, local(): lax.all_to_all(seg_keys[0], 'mem', split_axis=1, concat_axis=0, tiled=True)  21.7 us
    all_to_all x1, waiting for transfers between devices, local(): lax.all_to_all(seg_values[0], 'mem', split_axis=1, concat_axis=0, tiled=T...  19.3 us
    dot_general x4, matrix products, one_group(): jnp.einsum('gtk,gkd->gtd', weights, fetched_v, preferred_element_type=jnp...  17.6 us
    sub x4, matrix products, softmax_rows(): expo = jnp.exp(scores - highest)  16.9 us
  transfers between devices with their start and end apart: 6, of which 5 were waited for; matrix products, arithmetic and copies ran while one was open for 24% of the time, Pallas kernels for 0%

commit v1 on v0

v1 whole, which is shorter than its diff:
```python
import functools
import math

import jax
import jax.numpy as jnp
from jax import lax
from jax.experimental import pallas as pl
from jax.experimental.pallas import tpu as pltpu
from jax.sharding import PartitionSpec as P

HD = 128
BLK = 128
N = 16
SEG = N * BLK
PAIR = 2 * BLK
WIDE = 4 * BLK
LOW = -1e30
SCALE = math.log2(math.e) / math.sqrt(HD)
MESH = pl.DeviceIdType.MESH

OFFSETS = [8] + [x for d in range(7, 0, -1) for x in (d, N - d)]


def nt_dot(a, b):
    return lax.dot_general(a, b, (((1,), (1,)), ((), ())), preferred_element_type=jnp.float32)


def nn_dot(a, b):
    return jnp.dot(a, b, preferred_element_type=jnp.float32)


def rows_of(index, size):
    return pl.ds(pl.multiple_of(index * size, size), size)


def kernel(
    dims,
    pointer_ref, gate_ref, ids_ref, q_in, k_in, v_in, mk_in, mv_in, w_in, out_ref,
    qb, kb, vb, mkb, mvb, mk_both, mv_both, mk_old, mv_old, bias, scores,
    p_local, p_seg, p_old, base, mem_num, mem_den, sent, heads, wb, total,
    send_sem, recv_sem, own_sem, w_send, w_recv,
):
    ys, xs, cs = dims
    z = lax.axis_index("mem")
    dp = lax.axis_index("dp")
    core = lax.rem(dp, cs)
    x = lax.rem(dp // cs, xs)
    y = dp // (cs * xs)

    def at_z(offset):
        return lax.rem(z + offset, N)

    x_peers = [(y * xs + lax.rem(x + d, xs)) * cs + core for d in range(1, xs)]
    y_peers = [(lax.rem(y + d, ys) * xs + x) * cs + core for d in range(1, ys)]
    sibling = (y * xs + x) * cs + (1 - core)
    plane = x_peers + y_peers + [sibling]

    own = [
        pltpu.make_async_copy(mk_in.at[0, :, 0], mk_both, own_sem.at[0]),
        pltpu.make_async_copy(mv_in.at[0, :, 0], mv_both, own_sem.at[1]),
        pltpu.make_async_copy(q_in.at[0, :, rows_of(z, HD)], qb.at[rows_of(z, BLK)], own_sem.at[2]),
        pltpu.make_async_copy(k_in.at[0, :, rows_of(z, HD)], kb.at[rows_of(z, BLK)], own_sem.at[3]),
        pltpu.make_async_copy(v_in.at[0, :, rows_of(z, HD)], vb.at[rows_of(z, BLK)], own_sem.at[4]),
        pltpu.make_async_copy(w_in, wb.at[y * xs + x, core], own_sem.at[5]),
    ]
    for copy in own:
        copy.start()

    barrier = pltpu.get_barrier_semaphore()
    for o in OFFSETS:
        pl.semaphore_signal(barrier, inc=1, device_id={"mem": at_z(o)}, device_id_type=MESH)
    for peer in plane:
        pl.semaphore_signal(barrier, inc=1, device_id={"dp": peer}, device_id_type=MESH)
    pl.semaphore_wait(barrier, len(OFFSETS) + len(plane))

    def head_copy(a, o, src, dst):
        return pltpu.make_async_remote_copy(
            src_ref=src, dst_ref=dst, send_sem=send_sem.at[a, o], recv_sem=recv_sem.at[a, o],
            device_id={"mem": at_z(o)}, device_id_type=MESH,
        )

    def scatter(a, src, dst):
        copies = [
            head_copy(a, o, src.at[:, rows_of(at_z(o), HD)], dst.at[rows_of(z, BLK)])
            for o in OFFSETS
        ]
        for copy in copies:
            copy.start()
        return copies

    def w_copy(n, src, dst, peer):
        return pltpu.make_async_remote_copy(
            src_ref=src, dst_ref=dst, send_sem=w_send.at[n], recv_sem=w_recv.at[n],
            device_id={"dp": peer}, device_id_type=MESH,
        )

    w_first = [
        w_copy(n, w_in, wb.at[y * xs + x, core], peer) for n, peer in enumerate(x_peers)
    ]
    for copy in w_first:
        copy.start()
    q_copies = scatter(0, q_in.at[0], qb)
    k_copies = scatter(1, k_in.at[0], kb)

    pointer = pointer_ref[0]
    column = 1 - pointer // N

    def keep_old(both, old, copy):
        copy.wait()

        def step(r, _):
            old[rows_of(r, 16), :] = both[column, rows_of(r, 16), :]
            return 0

        lax.fori_loop(0, BLK // 16, step, 0)

    keep_old(mk_both, mk_old, own[0])
    mk_copies = scatter(2, mk_old, mkb)
    v_copies = scatter(3, v_in.at[0], vb)
    keep_old(mv_both, mv_old, own[1])
    mv_copies = scatter(4, mv_old, mvb)
    mkb[rows_of(z, BLK), :] = mk_old[:, rows_of(z, HD)]
    mvb[rows_of(z, BLK), :] = mv_old[:, rows_of(z, HD)]

    place = (ids_ref[0, :, 0, :] + pointer) & (2 * N - 1)
    block_of = lax.broadcasted_iota(jnp.int32, (N, WIDE), 1) // BLK
    for c in range(2 * N * BLK // WIDE):
        picked = jnp.full((N, WIDE), LOW, jnp.float32)
        for t in range(N):
            hit = (block_of + c * (WIDE // BLK)) == place[:, t : t + 1]
            picked = jnp.where(hit, 0.0, picked)
        bias[:, c * WIDE : (c + 1) * WIDE] = picked

    own[5].wait()
    for copy in w_first:
        copy.wait_recv()
    mine = wb.at[pl.ds(y * xs, xs), core]
    w_second = [w_copy(xs - 1 + n, mine, mine, peer) for n, peer in enumerate(y_peers)]
    for copy in w_second:
        copy.start()

    own[2].wait()
    own[3].wait()
    for copy in q_copies + k_copies:
        copy.wait_recv()

    def lane_max(m, s):
        for c in range(s.shape[1] // 128):
            m = jnp.maximum(m, s[:, c * 128 : (c + 1) * 128])
        return m

    def local_pair(i, _):
        q = qb[rows_of(i, PAIR), :]

        def first(j, m):
            s = nt_dot(q, kb[rows_of(j, PAIR), :]) * SCALE
            scores[:, rows_of(j, PAIR)] = s
            return lane_max(m, s)

        m = lax.fori_loop(0, i, first, jnp.full((PAIR, 128), LOW, jnp.float32))
        s = nt_dot(q, kb[rows_of(i, PAIR), :]) * SCALE
        row = lax.broadcasted_iota(jnp.int32, (PAIR, PAIR), 0)
        col = lax.broadcasted_iota(jnp.int32, (PAIR, PAIR), 1)
        s = jnp.where(row >= col, s, LOW)
        highest = jnp.max(lane_max(m, s), axis=1, keepdims=True)
        p_local[rows_of(i, PAIR), rows_of(i, PAIR)] = jnp.exp2(s - highest).astype(jnp.bfloat16)

        def second(j, _):
            p = jnp.exp2(scores[:, rows_of(j, PAIR)] - highest)
            p_local[rows_of(i, PAIR), rows_of(j, PAIR)] = p.astype(jnp.bfloat16)
            return 0

        lax.fori_loop(0, i, second, 0)
        return 0

    lax.fori_loop(0, N // 2, local_pair, 0)

    for copy in w_second:
        copy.wait_recv()
    half = wb.at[:, core]
    w_third = w_copy(xs + ys - 2, half, half, sibling)
    w_third.start()

    for copy in mk_copies:
        copy.wait_recv()

    def memory_pair(i, _):
        q = qb[rows_of(i, PAIR), :]

        def biased(s, at):
            return jnp.concatenate(
                [
                    s[:BLK] + bias[pl.ds(2 * i, 1), at],
                    s[BLK:] + bias[pl.ds(2 * i + 1, 1), at],
                ],
                axis=0,
            )

        m = jnp.full((PAIR, 128), LOW, jnp.float32)
        for c in range(SEG // WIDE):
            s = nt_dot(q, mkb[c * WIDE : (c + 1) * WIDE, :]) * SCALE
            s = biased(s, slice(SEG + c * WIDE, SEG + (c + 1) * WIDE))
            scores[:, SEG + c * WIDE : SEG + (c + 1) * WIDE] = s
            m = lane_max(m, s)

        def first(j, m):
            s = biased(nt_dot(q, kb[rows_of(j, PAIR), :]) * SCALE, rows_of(j, PAIR))
            scores[:, rows_of(j, PAIR)] = s
            return lane_max(m, s)

        m = lax.fori_loop(0, i + 1, first, m)
        highest = jnp.max(m, axis=1, keepdims=True)
        for c in range(SEG // WIDE):
            p = jnp.exp2(scores[:, SEG + c * WIDE : SEG + (c + 1) * WIDE] - highest)
            p_old[rows_of(i, PAIR), c * WIDE : (c + 1) * WIDE] = p.astype(jnp.bfloat16)

        def second(j, _):
            p = jnp.exp2(scores[:, rows_of(j, PAIR)] - highest)
            p_seg[rows_of(i, PAIR), rows_of(j, PAIR)] = p.astype(jnp.bfloat16)
            return 0

        lax.fori_loop(0, i + 1, second, 0)
        return 0

    lax.fori_loop(0, N // 2, memory_pair, 0)

    own[4].wait()
    for copy in v_copies:
        copy.wait_recv()
    gate = 1.0 / (1.0 + jnp.exp(jnp.full((8, 128), -gate_ref[0], jnp.float32)))[:1]
    ones = jnp.ones((PAIR, 128), jnp.bfloat16)

    def value_pair(i, _):
        def step(j, acc):
            values = jnp.concatenate([vb[rows_of(j, PAIR), :], ones], axis=1)
            p = jnp.concatenate(
                [
                    p_local[rows_of(i, PAIR), rows_of(j, PAIR)],
                    p_seg[rows_of(i, PAIR), rows_of(j, PAIR)],
                ],
                axis=0,
            )
            return acc + nn_dot(p, values)

        acc = lax.fori_loop(0, i + 1, step, jnp.zeros((2 * PAIR, PAIR), jnp.float32))
        base[rows_of(i, PAIR), :] = (1.0 - gate) * (acc[:PAIR, :128] / acc[:PAIR, 128:])
        mem_num[rows_of(i, PAIR), :] = acc[PAIR:, :128]
        mem_den[rows_of(i, PAIR), :] = acc[PAIR:, 128:]
        return 0

    lax.fori_loop(0, N // 2, value_pair, 0)

    for copy in mv_copies:
        copy.wait_recv()

    def finish(o):
        i = at_z(o)
        rows = rows_of(i, BLK)
        values = jnp.concatenate([mvb[...], jnp.ones((SEG, 128), jnp.bfloat16)], axis=1)
        got = nn_dot(p_old[rows, :], values)
        memory = (got[:, :128] + mem_num[rows, :]) / (got[:, 128:] + mem_den[rows, :])
        return (gate * memory + base[rows, :]).astype(jnp.bfloat16)

    out_copies = []
    for n, o in enumerate(OFFSETS):
        sent[n] = finish(o)
        copy = head_copy(5, o, sent.at[n], heads.at[z])
        copy.start()
        out_copies.append(copy)
    heads[z] = finish(0)

    w_third.wait_recv()

    def weights(h):
        return wb[h].reshape(HD, wb.shape[-1])

    total[...] = nn_dot(heads[z], weights(z))
    for n, o in enumerate(OFFSETS):
        out_copies[n].wait_recv()
        h = at_z(N - o)
        if n < len(OFFSETS) - 1:
            total[...] += nn_dot(heads[h], weights(h))
        else:
            out_ref[0] = (total[...] + nn_dot(heads[h], weights(h))).astype(jnp.bfloat16)

    for copy in w_first + w_second + [w_third]:
        copy.wait_send()
    for copy in q_copies + k_copies + mk_copies + v_copies + mv_copies + out_copies:
        copy.wait_send()


def local(
    dims,
    queries, seg_keys, seg_values, mem_keys, mem_values, block_ids, pointer, gate_bias, out_weight,
):
    width = queries.shape[2]
    ys, xs, cs = dims
    bf16, f32 = jnp.bfloat16, jnp.float32
    vmem, smem, hbm = (
        pl.BlockSpec(memory_space=pltpu.VMEM),
        pl.BlockSpec(memory_space=pltpu.SMEM),
        pl.BlockSpec(memory_space=pl.ANY),
    )
    n_plane = xs + ys - 1
    return pl.pallas_call(
        functools.partial(kernel, dims),
        out_shape=jax.ShapeDtypeStruct(queries.shape, bf16),
        in_specs=[smem, smem, vmem, hbm, hbm, hbm, hbm, hbm, hbm],
        out_specs=vmem,
        scratch_shapes=[
            *[pltpu.VMEM((SEG, HD), bf16) for _ in range(5)],
            pltpu.VMEM((2, BLK, width), bf16),
            pltpu.VMEM((2, BLK, width), bf16),
            pltpu.VMEM((BLK, width), bf16),
            pltpu.VMEM((BLK, width), bf16),
            pltpu.VMEM((N, 2 * SEG), f32),
            pltpu.VMEM((PAIR, 2 * SEG), f32),
            pltpu.VMEM((SEG, SEG), bf16),
            pltpu.VMEM((SEG, SEG), bf16),
            pltpu.VMEM((SEG, SEG), bf16),
            pltpu.VMEM((SEG, HD), f32),
            pltpu.VMEM((SEG, HD), f32),
            pltpu.VMEM((SEG, HD), f32),
            pltpu.VMEM((N - 1, BLK, HD), bf16),
            pltpu.VMEM((N, BLK, HD), bf16),
            pltpu.VMEM((ys * xs, cs, *out_weight.shape), bf16),
            pltpu.VMEM((BLK, width), f32),
            pltpu.SemaphoreType.DMA((6, N)),
            pltpu.SemaphoreType.DMA((6, N)),
            pltpu.SemaphoreType.DMA((6,)),
            pltpu.SemaphoreType.DMA((n_plane,)),
            pltpu.SemaphoreType.DMA((n_plane,)),
        ],
        compiler_params=pltpu.CompilerParams(
            collective_id=0, has_side_effects=True, vmem_limit_bytes=60 * 1024 * 1024
        ),
        cost_estimate=pl.CostEstimate(
            flops=5_000_000_000, bytes_accessed=5_000_000, transcendentals=9_000_000
        ),
    )(pointer, gate_bias, block_ids, queries, seg_keys, seg_values, mem_keys, mem_values, out_weight)


def solution(mesh):
    dims = (4, 4, 2)
    in_specs = (
        P("dp", "mem", None),
        P("dp", "mem", None),
        P("dp", "mem", None),
        P("dp", None, "mem", None, None),
        P("dp", None, "mem", None, None),
        P("dp", None, "mem", None),
        P("dp"),
        P("mem"),
        P("dp", None),
    )
    return jax.shard_map(
        functools.partial(local, dims), mesh=mesh, in_specs=in_specs,
        out_specs=P("dp", "mem", None), check_vma=False,
    )
```

time: 346 us -> 161 us (0.47); the launches traced: 340 us -> 161 us
  Pallas kernels: 0 us -> 158 us
  waiting for transfers between devices: 128 us -> 0 us
  starting transfers between devices: 66.7 us -> 0 us
  matrix products: 48.8 us -> 0 us
  local copies, waits for them, and re-layouts: 37.7 us -> 1.88 us
  blocking collectives: 35.4 us -> 0 us
  between operations: 15.1 us -> 1.3 us
  other arithmetic: 8.09 us -> 0 us
    pallas_call x0 -> x1, Pallas kernels: none -> 158 us  [local(): pl.pallas_call(functools.partial(kernel, dims), out_shape=jax.ShapeDtypeS...]
    all_to_all x5 -> x0, waiting for transfers between devices: 127 us -> none  [the longest x1 33.5 us: local(): lax.all_to_all(mem_keys[0, :, 0].reshape(slots_here * BLK, model_width),...]
    all_to_all x5 -> x0, starting transfers between devices: 66.6 us -> none  [the longest x1 15.7 us: local(): lax.all_to_all(queries[0], 'mem', split_axis=1, concat_axis=0, tiled=True)]
    all_to_all x1 -> x0, blocking collectives: 35.4 us -> none  [local(): lax.all_to_all(attended_heads, 'mem', split_axis=0, concat_axis=1, tiled=...]
    dot_general x13 -> x0, matrix products: 31.8 us -> none  [the longest x4 17.6 us: one_group(): jnp.einsum('gtk,gkd->gtd', weights, fetched_v, preferred_element_type=jnp...]
    gather x8 -> x0, local copies, waits for them, and re-layouts: 17.3 us -> none  [the longest x4 13.5 us: one_group(): fetched_v = memv_h[slot_part].reshape(group, -1, HD)]
    sub x4 -> x0, matrix products: 16.9 us -> none  [softmax_rows(): expo = jnp.exp(scores - highest)]
    all_to_all x5 -> x0, local copies, waits for them, and re-layouts: 5.32 us -> none  [the longest x1 1.27 us: local(): lax.all_to_all(mem_keys[0, :, 0].reshape(slots_here * BLK, model_width),...]
  transfers between devices with their start and end apart: 6 -> 0, of which waited for: 5 -> 0; matrix products, arithmetic and copies ran while one was open for 24% -> 0% of each run, Pallas kernels for 0% -> 0%
where the time goes in v1:
time: 161 us
  Pallas kernels  158 us (98%)
  local copies, waits for them, and re-layouts  1.88 us (1%)
    pallas_call x1, Pallas kernels, local(): pl.pallas_call(functools.partial(kernel, dims), out_shape=jax.ShapeDtypeS...  158 us

profile of v1, /device:TPU:1, one launch (start us, length us, event | category | flops | bytes accessed | tf_op | source)
XLA Modules:
  0.0 161.3 jit_solution(9753106171912888367)
XLA Ops:
  1.3 158.1 %shard_map.91 = bf16[1,128,2048]{2,1,0:T(8,128)(2,1)} custom-call(s32[1]{0:T(128)S(6)} %copy.11.pointer_ref, f32[1]{0:T(128)S(6)} %copy.12.gate_ref, s32[1,16,1,16]{3,2,1,0:T(1,128)} %ids_ref.1, bf16[1,128,2048]{2,1,0:T(8,128)(2,1)} %q_in.1, bf16[1,128,2048]{2,1,0:T(8,128)(2,1)} %k_in.1, bf16[1,128,2048]{2,1,0:T(8,128)(2,1)} %v_in.1, ...), custom_call_target="tpu_custom_call" | custom-call | flops 5000000000 | bytes 5000000 | tf_op jit(solution)/shard_map/pallas_call | solution.py:305
  159.4 1.9 %copy.13 = bf16[1,128,2048]{2,1,0:T(8,128)(2,1)} copy(bf16[1,128,2048]{2,1,0:T(8,128)(2,1)} %shard_map.91) | data formatting | bytes 1048576

commit v2 on v1

--- a/solution.py
+++ b/solution.py
@@ -35,8 +35,8 @@
 
 def kernel(
     dims,
-    pointer_ref, gate_ref, ids_ref, q_in, k_in, v_in, mk_in, mv_in, w_in, out_ref,
-    qb, kb, vb, mkb, mvb, mk_both, mv_both, mk_old, mv_old, bias, scores,
+    pointer_in, gate_in, ids_in, q_in, k_in, v_in, mk_in, mv_in, w_in, out_ref,
+    pointer_ref, gate_ref, ids_ref, qb, kb, vb, mkb, mvb, mk_both, mv_both, mk_old, mv_old, bias, scores,
     p_local, p_seg, p_old, base, mem_num, mem_den, sent, heads, wb, total,
     send_sem, recv_sem, own_sem, w_send, w_recv,
 ):
@@ -62,6 +62,9 @@
         pltpu.make_async_copy(k_in.at[0, :, rows_of(z, HD)], kb.at[rows_of(z, BLK)], own_sem.at[3]),
         pltpu.make_async_copy(v_in.at[0, :, rows_of(z, HD)], vb.at[rows_of(z, BLK)], own_sem.at[4]),
         pltpu.make_async_copy(w_in, wb.at[y * xs + x, core], own_sem.at[5]),
+        pltpu.make_async_copy(pointer_in, pointer_ref, own_sem.at[6]),
+        pltpu.make_async_copy(gate_in, gate_ref, own_sem.at[7]),
+        pltpu.make_async_copy(ids_in, ids_ref, own_sem.at[8]),
     ]
     for copy in own:
         copy.start()
@@ -102,6 +105,7 @@
     q_copies = scatter(0, q_in.at[0], qb)
     k_copies = scatter(1, k_in.at[0], kb)
 
+    own[6].wait()
     pointer = pointer_ref[0]
     column = 1 - pointer // N
 
@@ -122,6 +126,7 @@
     mkb[rows_of(z, BLK), :] = mk_old[:, rows_of(z, HD)]
     mvb[rows_of(z, BLK), :] = mv_old[:, rows_of(z, HD)]
 
+    own[8].wait()
     place = (ids_ref[0, :, 0, :] + pointer) & (2 * N - 1)
     block_of = lax.broadcasted_iota(jnp.int32, (N, WIDE), 1) // BLK
     for c in range(2 * N * BLK // WIDE):
@@ -227,6 +232,7 @@
     own[4].wait()
     for copy in v_copies:
         copy.wait_recv()
+    own[7].wait()
     gate = 1.0 / (1.0 + jnp.exp(jnp.full((8, 128), -gate_ref[0], jnp.float32)))[:1]
     ones = jnp.ones((PAIR, 128), jnp.bfloat16)
 
@@ -296,18 +302,17 @@
     width = queries.shape[2]
     ys, xs, cs = dims
     bf16, f32 = jnp.bfloat16, jnp.float32
-    vmem, smem, hbm = (
-        pl.BlockSpec(memory_space=pltpu.VMEM),
-        pl.BlockSpec(memory_space=pltpu.SMEM),
-        pl.BlockSpec(memory_space=pl.ANY),
-    )
+    hbm = pl.BlockSpec(memory_space=pltpu.HBM)
     n_plane = xs + ys - 1
     return pl.pallas_call(
         functools.partial(kernel, dims),
-        out_shape=jax.ShapeDtypeStruct(queries.shape, bf16),
-        in_specs=[smem, smem, vmem, hbm, hbm, hbm, hbm, hbm, hbm],
-        out_specs=vmem,
+        out_shape=pltpu.VMEM(queries.shape, bf16),
+        in_specs=[hbm] * 9,
+        out_specs=pl.BlockSpec(memory_space=pltpu.VMEM),
         scratch_shapes=[
+            pltpu.SMEM(pointer.shape, jnp.int32),
+            pltpu.SMEM(gate_bias.shape, f32),
+            pltpu.VMEM(block_ids.shape, jnp.int32),
             *[pltpu.VMEM((SEG, HD), bf16) for _ in range(5)],
             pltpu.VMEM((2, BLK, width), bf16),
             pltpu.VMEM((2, BLK, width), bf16),
@@ -327,7 +332,7 @@
             pltpu.VMEM((BLK, width), f32),
             pltpu.SemaphoreType.DMA((6, N)),
             pltpu.SemaphoreType.DMA((6, N)),
-            pltpu.SemaphoreType.DMA((6,)),
+            pltpu.SemaphoreType.DMA((9,)),
             pltpu.SemaphoreType.DMA((n_plane,)),
             pltpu.SemaphoreType.DMA((n_plane,)),
         ],

time: 161 us -> 159 us (0.988)
  no operation moved by 1% of the time
where the time goes in v2:
time: 159 us
  Pallas kernels  157 us (99%)
    pallas_call x1, Pallas kernels, local(): pl.pallas_call(functools.partial(kernel, dims), out_shape=pltpu.VMEM(quer...  157 us

profile of v2, /device:TPU:1, one launch (start us, length us, event | category | flops | bytes accessed | tf_op | source)
XLA Modules:
  0.0 158.8 jit_solution(12670324937336187168)
XLA Ops:
  1.3 156.7 %shard_map.91 = bf16[1,128,2048]{2,1,0:T(8,128)(2,1)S(1)} custom-call(s32[1]{0:T(128)S(6)} %copy.12.pointer_in, f32[1]{0:T(128)S(6)} %copy.13.gate_in, s32[1,16,1,16]{3,2,1,0:T(1,128)} %ids_in.1, bf16[1,128,2048]{2,1,0:T(8,128)(2,1)} %q_in.1, bf16[1,128,2048]{2,1,0:T(8,128)(2,1)} %k_in.1, bf16[1,128,2048]{2,1,0:T(8,128)(2,1)} %v_in.1, ...), custom_call_target="tpu_custom_call" | custom-call | flops 5000000000 | bytes 5000000 | tf_op jit(solution)/shard_map/pallas_call | solution.py:307
  158.0 0.8 copy.11

commit v3 on v2

v3 whole, which is shorter than its diff:
```python
import functools
import math

import jax
import jax.numpy as jnp
from jax import lax
from jax.experimental import pallas as pl
from jax.experimental.pallas import tpu as pltpu
from jax.sharding import PartitionSpec as P

HD = 128
BLK = 128
N = 16
HALF = N // 2
SEG = N * BLK
KEYS = HALF * BLK
PAIR = 2 * BLK
WIDE = 4 * BLK
LOW = -1e30
LOG2E = math.log2(math.e)
SCALE = LOG2E / math.sqrt(HD)
MESH = pl.DeviceIdType.MESH

GAP = 3
LEFT = 6
ROLES = (0, 1)


def offset(role, w):
    return LEFT - w if role == 0 else LEFT + GAP - HALF - w


def head_shift(role):
    return 0 if role == 0 else -GAP


FAR_FIRST = sorted(
    [(role, w) for role in ROLES for w in range(HALF) if offset(role, w)],
    key=lambda rw: -abs(offset(*rw)),
)
OWN = [(role, w) for role in ROLES for w in range(HALF) if offset(role, w) == 0]
PEERS = sorted({offset(*rw) for rw in FAR_FIRST} | {GAP, -GAP})


def nt_dot(a, b):
    return lax.dot_general(a, b, (((1,), (1,)), ((), ())), preferred_element_type=jnp.float32)


def nn_dot(a, b):
    return jnp.dot(a, b, preferred_element_type=jnp.float32)


def rows_of(index, size):
    return pl.ds(pl.multiple_of(index * size, size), size)


def log2(x):
    return jnp.log(x) * LOG2E


def join(a, b):
    m = jnp.maximum(a, b)
    return m + log2(jnp.exp2(a - m) + jnp.exp2(b - m))


def kernel(
    dims,
    pointer_in, gate_in, ids_in, q_in, k_in, v_in, mk_in, mv_in, w_in, out_ref,
    pointer_ref, gate_ref, ids, gates, qb, kb, vb, mkb, mvb, mk_both, mv_both, mk_old, mv_old,
    bias, scores, p_loc, p_seg, p_old, parts, stats, lines, lse_out, lse_in, part_out, part_in,
    sent, heads, wb, total,
    send_sem, recv_sem, out_send, out_recv, part_send, part_recv, pass_send, pass_recv,
    own_sem, w_send, w_recv,
):
    ys, xs, cs = dims
    z = lax.axis_index("mem")
    dp = lax.axis_index("dp")
    core = lax.rem(dp, cs)
    x = lax.rem(dp // cs, xs)
    y = dp // (cs * xs)

    def at_z(o):
        return lax.rem(z + (o + N), N)

    x_peers = [(y * xs + lax.rem(x + d, xs)) * cs + core for d in range(1, xs)]
    y_peers = [(lax.rem(y + d, ys) * xs + x) * cs + core for d in range(1, ys)]
    sibling = (y * xs + x) * cs + (1 - core)
    plane = x_peers + y_peers + [sibling]

    singles = [
        pltpu.make_async_copy(mk_in.at[0, :, 0], mk_both, own_sem.at[0]),
        pltpu.make_async_copy(mv_in.at[0, :, 0], mv_both, own_sem.at[1]),
        pltpu.make_async_copy(w_in, wb.at[y * xs + x, core], own_sem.at[2]),
        pltpu.make_async_copy(pointer_in, pointer_ref, own_sem.at[3]),
        pltpu.make_async_copy(gate_in, gate_ref, own_sem.at[4]),
        pltpu.make_async_copy(ids_in.at[0, :, 0], ids.at[0], own_sem.at[5]),
    ]

    def own_copies(n, src, dst, q):
        copies = []
        for role, w in OWN:
            row = w + (HALF * role if q else 0)
            copies.append(
                pltpu.make_async_copy(
                    src.at[0, :, rows_of(at_z(head_shift(role)), HD)],
                    dst.at[role, row * BLK : (row + 1) * BLK],
                    own_sem.at[n + role],
                )
            )
        return copies

    own_q, own_k = own_copies(6, q_in, qb, True), own_copies(8, k_in, kb, False)
    own_v = own_copies(10, v_in, vb, False)
    for copy in singles + own_q + own_k + own_v:
        copy.start()

    barrier = pltpu.get_barrier_semaphore()
    for o in PEERS:
        pl.semaphore_signal(barrier, inc=1, device_id={"mem": at_z(o)}, device_id_type=MESH)
    for peer in plane:
        pl.semaphore_signal(barrier, inc=1, device_id={"dp": peer}, device_id_type=MESH)
    pl.semaphore_wait(barrier, len(PEERS) + len(plane))

    def along_z(o, src, dst, sent_to, got):
        return pltpu.make_async_remote_copy(
            src_ref=src, dst_ref=dst, send_sem=sent_to, recv_sem=got,
            device_id={"mem": at_z(o)}, device_id_type=MESH,
        )

    def scatter(a, src, dst, q=False):
        copies = []
        for role, w in FAR_FIRST:
            o = offset(role, w)
            row = w + (HALF * role if q else 0)
            copy = along_z(
                o, src.at[:, rows_of(at_z(o + head_shift(role)), HD)],
                dst.at[role, row * BLK : (row + 1) * BLK],
                send_sem.at[a, role, w], recv_sem.at[a, role, w],
            )
            copy.start()
            copies.append(copy)
        return copies

    def w_copy(n, src, dst, peer):
        return pltpu.make_async_remote_copy(
            src_ref=src, dst_ref=dst, send_sem=w_send.at[n], recv_sem=w_recv.at[n],
            device_id={"dp": peer}, device_id_type=MESH,
        )

    w_first = [
        w_copy(n, w_in, wb.at[y * xs + x, core], peer) for n, peer in enumerate(x_peers)
    ]
    for copy in w_first:
        copy.start()
    q_copies = scatter(0, q_in.at[0], qb, q=True)
    k_copies = scatter(1, k_in.at[0], kb)

    singles[4].wait()
    gates[0] = jnp.full((8, 128), gate_ref[0], jnp.float32)
    singles[5].wait()
    ids_copy = along_z(GAP, ids.at[0], ids.at[1], pass_send.at[4], pass_recv.at[4])
    gate_copy = along_z(GAP, gates.at[0], gates.at[1], pass_send.at[5], pass_recv.at[5])
    ids_copy.start()
    gate_copy.start()

    singles[3].wait()
    pointer = pointer_ref[0]
    column = 1 - pointer // N

    def keep_old(both, old, copy):
        copy.wait()

        def step(r, _):
            old[rows_of(r, 16), :] = both[column, rows_of(r, 16), :]
            return 0

        lax.fori_loop(0, BLK // 16, step, 0)

    keep_old(mk_both, mk_old, singles[0])
    keep_old(mv_both, mv_old, singles[1])
    for role, w in OWN:
        columns = rows_of(at_z(head_shift(role)), HD)
        mkb[role, w * BLK : (w + 1) * BLK] = mk_old[:, columns]
        mvb[role, w * BLK : (w + 1) * BLK] = mv_old[:, columns]

    for copy in own_q:
        copy.wait()
    for copy in q_copies:
        copy.wait_recv()
    near, far = slice(0, KEYS), slice(KEYS, SEG)
    relays = [
        along_z(GAP, qb.at[0, near], qb.at[1, near], pass_send.at[0], pass_recv.at[0]),
        along_z(-GAP, qb.at[1, far], qb.at[0, far], pass_send.at[1], pass_recv.at[1]),
    ]
    for copy in relays:
        copy.start()
    mk_copies = scatter(2, mk_old, mkb)
    v_copies = scatter(3, v_in.at[0], vb)
    mv_copies = scatter(4, mv_old, mvb)

    def block_at(role, u):
        return (z + u + (N - LEFT + head_shift(role))) & (N - 1)

    ids_copy.wait_recv()
    gate_copy.wait_recv()
    for role in ROLES:
        place = (ids[role] + pointer) & (2 * N - 1)
        for c in range(2 * KEYS // WIDE):
            w = lax.broadcasted_iota(jnp.int32, (N, WIDE), 1) // BLK + c * (WIDE // BLK)
            old = jnp.where(w >= HALF, N, 0)
            block = block_at(role, (w & (HALF - 1)) + HALF * role) + old
            picked = jnp.full((N, WIDE), LOW, jnp.float32)
            for t in range(N):
                picked = jnp.where(block == place[:, t : t + 1], 0.0, picked)
            bias[role, :, c * WIDE : (c + 1) * WIDE] = picked

    singles[2].wait()
    for copy in w_first:
        copy.wait_recv()
    mine = wb.at[pl.ds(y * xs, xs), core]
    w_second = [w_copy(xs - 1 + n, mine, mine, peer) for n, peer in enumerate(y_peers)]
    for copy in w_second:
        copy.start()

    def lane_max(m, s):
        for c in range(s.shape[1] // 128):
            m = jnp.maximum(m, s[:, c * 128 : (c + 1) * 128])
        return m

    def lane_sum(s):
        acc = s[:, :128]
        for c in range(1, s.shape[1] // 128):
            acc = acc + s[:, c * 128 : (c + 1) * 128]
        return acc

    chunks = range(KEYS // WIDE)

    def span(c):
        return slice(c * WIDE, (c + 1) * WIDE)

    def weigh(role, i, at, m, target, lane):
        highest = jnp.max(m, axis=1, keepdims=True)
        acc = jnp.zeros((PAIR, 128), jnp.float32)
        for c in chunks:
            p = jnp.exp2(scores[:, at + c * WIDE : at + (c + 1) * WIDE] - highest)
            target[role, rows_of(i, PAIR), span(c)] = p.astype(jnp.bfloat16)
            acc = acc + lane_sum(p)
        stats[role, rows_of(i, PAIR), lane : lane + 1] = highest
        stats[role, rows_of(i, PAIR), lane + 1 : lane + 2] = jnp.sum(acc, axis=1, keepdims=True)

    def picked_only(role, i, s, at):
        rows = [bias[role, pl.ds(block_at(role, 2 * i + b), 1), at] for b in (0, 1)]
        return jnp.concatenate([s[:BLK] + rows[0], s[BLK:] + rows[1]], axis=0)

    def segment_pair(role):
        def body(i, _):
            q = qb[role, rows_of(i, PAIR), :]
            row = lax.broadcasted_iota(jnp.int32, (PAIR, 128), 0)
            q_token = block_at(role, 2 * i + row // BLK) * BLK + (row & (BLK - 1))
            m_loc = m_seg = jnp.full((PAIR, 128), LOW, jnp.float32)
            for c in chunks:
                s = nt_dot(q, kb[role, span(c), :]) * SCALE
                kept = []
                for b in range(WIDE // BLK):
                    w = c * (WIDE // BLK) + b + HALF * role
                    lane = lax.broadcasted_iota(jnp.int32, (PAIR, 128), 1)
                    k_token = block_at(role, w) * BLK + lane
                    kept.append(
                        jnp.where(q_token >= k_token, s[:, b * BLK : (b + 1) * BLK], LOW)
                    )
                kept = jnp.concatenate(kept, axis=1)
                scores[:, span(c)] = kept
                m_loc = lane_max(m_loc, kept)
                s = picked_only(role, i, s, span(c))
                scores[:, KEYS + c * WIDE : KEYS + (c + 1) * WIDE] = s
                m_seg = lane_max(m_seg, s)
            weigh(role, i, 0, m_loc, p_loc, 0)
            weigh(role, i, KEYS, m_seg, p_seg, 2)
            return 0

        return body

    def old_pair(role):
        def body(i, _):
            q = qb[role, rows_of(i, PAIR), :]
            m_old = jnp.full((PAIR, 128), LOW, jnp.float32)
            for c in chunks:
                s = nt_dot(q, mkb[role, span(c), :]) * SCALE
                s = picked_only(role, i, s, slice(KEYS + c * WIDE, KEYS + (c + 1) * WIDE))
                scores[:, span(c)] = s
                m_old = lane_max(m_old, s)
            weigh(role, i, 0, m_old, p_old, 4)
            return 0

        return body

    for copy in own_k:
        copy.wait()
    for copy in k_copies:
        copy.wait_recv()
    quarter = HALF // 2
    lax.fori_loop(0, quarter, segment_pair(0), 0)
    lax.fori_loop(quarter, HALF, segment_pair(1), 0)
    relays[1].wait_recv()
    lax.fori_loop(quarter, HALF, segment_pair(0), 0)
    relays[0].wait_recv()
    lax.fori_loop(0, quarter, segment_pair(1), 0)

    for copy in w_second:
        copy.wait_recv()
    half = wb.at[:, core]
    w_third = w_copy(xs + ys - 2, half, half, sibling)
    w_third.start()

    for copy in mk_copies:
        copy.wait_recv()
    for role in ROLES:
        lax.fori_loop(0, HALF, old_pair(role), 0)

    for role in ROLES:
        for u in range(N):
            turned = jnp.transpose(stats[role, u * BLK : (u + 1) * BLK, :])
            for n in range(6):
                lines[role, n, u : u + 1, :] = turned[n : n + 1]
        loc, seg, old = (lines[role, n] + log2(lines[role, n + 1]) for n in (0, 2, 4))
        lse_out[role, 0] = loc
        lse_out[role, 1] = join(seg, old)
    lse_copies = [
        along_z(GAP, lse_out.at[0], lse_in.at[1], pass_send.at[2], pass_recv.at[2]),
        along_z(-GAP, lse_out.at[1], lse_in.at[0], pass_send.at[3], pass_recv.at[3]),
    ]
    for copy in lse_copies:
        copy.start()

    for copy in own_v:
        copy.wait()
    for copy in v_copies:
        copy.wait_recv()

    def value_pair(role):
        def body(i, _):
            rows = rows_of(i, PAIR)
            p = jnp.concatenate([p_loc[role, rows, :], p_seg[role, rows, :]], axis=0)
            acc = nn_dot(p, vb[role])
            parts[role, 0, rows, :] = acc[:PAIR]
            parts[role, 1, rows, :] = acc[PAIR:]
            return 0

        return body

    for role in ROLES:
        lax.fori_loop(0, HALF, value_pair(role), 0)

    for copy in mv_copies:
        copy.wait_recv()

    for copy in lse_copies:
        copy.wait_recv()
    factors = []
    for role in ROLES:
        gate = 1.0 / (1.0 + jnp.exp(-gates[role, :1, :1]))
        all_loc = join(lse_out[role, 0], lse_in[role, 0])
        all_mem = join(lse_out[role, 1], lse_in[role, 1])
        factors.append(
            [
                (1.0 - gate) * jnp.exp2(lines[role, 0] - all_loc),
                gate * jnp.exp2(lines[role, 2] - all_mem),
                gate * jnp.exp2(lines[role, 4] - all_mem),
            ]
        )

    def finish(role, u):
        rows = slice(u * BLK, (u + 1) * BLK)
        block = jnp.concatenate(
            [f[u : u + 1] for f in factors[role]] + [jnp.zeros((125, 128), jnp.float32)], axis=0
        )
        columns = jnp.transpose(block)
        got = nn_dot(p_old[role, rows, :], mvb[role])
        return (
            columns[:, 0:1] * parts[role, 0, rows, :]
            + columns[:, 1:2] * parts[role, 1, rows, :]
            + columns[:, 2:3] * got
        )

    order = [w for d in range(quarter) for w in (d, HALF - 1 - d)]
    part_copies = {}
    for w in order:
        for role in ROLES:
            part_out[role, w] = finish(role, w + HALF * (1 - role)).astype(jnp.bfloat16)
            copy = along_z(
                GAP if role == 0 else -GAP, part_out.at[role, w], part_in.at[1 - role, w],
                part_send.at[role, w], part_recv.at[1 - role, w],
            )
            copy.start()
            part_copies[role, w] = copy

    out_copies = {}
    for w in order:
        for role in ROLES:
            mine_f32 = finish(role, w + HALF * role)
            part_copies[1 - role, w].wait_recv()
            done = (mine_f32 + part_in[role, w].astype(jnp.float32)).astype(jnp.bfloat16)
            h = at_z(head_shift(role))
            o = -offset(role, w)
            if o == 0:
                heads[h] = done
            else:
                sent[role, w] = done
                copy = along_z(
                    o, sent.at[role, w], heads.at[h], out_send.at[role, w], out_recv.at[role, w]
                )
                copy.start()
                out_copies[role, w] = copy

    w_third.wait_recv()

    def weights(h):
        return wb[h].reshape(HD, wb.shape[-1])

    steps = [(role, w) for w in order for role in ROLES]
    for n, (role, w) in enumerate(steps):
        if (role, w) in out_copies:
            out_copies[role, w].wait_recv()
        h = at_z(LEFT - (w + HALF * role))
        term = nn_dot(heads[h], weights(h))
        if n == 0:
            total[...] = term
        elif n < len(steps) - 1:
            total[...] += term
        else:
            out_ref[0] = (total[...] + term).astype(jnp.bfloat16)

    for copy in w_first + w_second + [w_third]:
        copy.wait_send()
    for copy in q_copies + k_copies + mk_copies + v_copies + mv_copies + relays + lse_copies:
        copy.wait_send()
    for copy in [ids_copy, gate_copy, *part_copies.values(), *out_copies.values()]:
        copy.wait_send()


def local(
    dims,
    queries, seg_keys, seg_values, mem_keys, mem_values, block_ids, pointer, gate_bias, out_weight,
):
    width = queries.shape[2]
    ys, xs, cs = dims
    bf16, f32, i32 = jnp.bfloat16, jnp.float32, jnp.int32
    hbm = pl.BlockSpec(memory_space=pltpu.HBM)
    n_plane = xs + ys - 1
    dma = pltpu.SemaphoreType.DMA
    return pl.pallas_call(
        functools.partial(kernel, dims),
        out_shape=pltpu.VMEM(queries.shape, bf16),
        in_specs=[hbm] * 9,
        out_specs=pl.BlockSpec(memory_space=pltpu.VMEM),
        scratch_shapes=[
            pltpu.SMEM(pointer.shape, i32),
            pltpu.SMEM(gate_bias.shape, f32),
            pltpu.VMEM((2, N, N), i32),
            pltpu.VMEM((2, 8, 128), f32),
            pltpu.VMEM((2, SEG, HD), bf16),
            *[pltpu.VMEM((2, KEYS, HD), bf16) for _ in range(4)],
            pltpu.VMEM((2, BLK, width), bf16),
            pltpu.VMEM((2, BLK, width), bf16),
            pltpu.VMEM((BLK, width), bf16),
            pltpu.VMEM((BLK, width), bf16),
            pltpu.VMEM((2, N, 2 * KEYS), f32),
            pltpu.VMEM((PAIR, 2 * KEYS), f32),
            *[pltpu.VMEM((2, SEG, KEYS), bf16) for _ in range(3)],
            pltpu.VMEM((2, 2, SEG, HD), f32),
            pltpu.VMEM((2, SEG, 128), f32),
            pltpu.VMEM((2, 6, N, 128), f32),
            pltpu.VMEM((2, 2, N, 128), f32),
            pltpu.VMEM((2, 2, N, 128), f32),
            *[pltpu.VMEM((2, HALF, BLK, HD), bf16) for _ in range(3)],
            pltpu.VMEM((N, BLK, HD), bf16),
            pltpu.VMEM((ys * xs, cs, *out_weight.shape), bf16),
            pltpu.VMEM((BLK, width), f32),
            dma((5, 2, HALF)),
            dma((5, 2, HALF)),
            *[dma((2, HALF)) for _ in range(4)],
            dma((6,)),
            dma((6,)),
            dma((12,)),
            dma((n_plane,)),
            dma((n_plane,)),
        ],
        compiler_params=pltpu.CompilerParams(
            collective_id=0, has_side_effects=True, vmem_limit_bytes=60 * 1024 * 1024
        ),
        cost_estimate=pl.CostEstimate(
            flops=5_000_000_000, bytes_accessed=5_000_000, transcendentals=9_000_000
        ),
    )(pointer, gate_bias, block_ids, queries, seg_keys, seg_values, mem_keys, mem_values, out_weight)


def solution(mesh):
    dims = (4, 4, 2)
    in_specs = (
        P("dp", "mem", None),
        P("dp", "mem", None),
        P("dp", "mem", None),
        P("dp", None, "mem", None, None),
        P("dp", None, "mem", None, None),
        P("dp", None, "mem", None),
        P("dp"),
        P("mem"),
        P("dp", None),
    )
    return jax.shard_map(
        functools.partial(local, dims), mesh=mesh, in_specs=in_specs,
        out_specs=P("dp", "mem", None), check_vma=False,
    )
```

time: 159 us -> 153 us (0.962)
  Pallas kernels: 157 us -> 149 us
    pallas_call x1, Pallas kernels: 157 us -> 149 us  [local(): pl.pallas_call(functools.partial(kernel, dims), out_shape=pltpu.VMEM(quer...]
where the time goes in v3:
time: 153 us; the launch traced here: 151 us
  Pallas kernels  149 us (97%)
    pallas_call x1, Pallas kernels, local(): pl.pallas_call(functools.partial(kernel, dims), out_shape=pltpu.VMEM(quer...  149 us

profile of v3, /device:TPU:1, one launch (start us, length us, event | category | flops | bytes accessed | tf_op | source)
XLA Modules:
  0.0 151.3 jit_solution(12886971530521028562)
XLA Ops:
  1.3 149.2 %shard_map.91 = bf16[1,128,2048]{2,1,0:T(8,128)(2,1)S(1)} custom-call(s32[1]{0:T(128)S(6)} %copy.12.pointer_in, f32[1]{0:T(128)S(6)} %copy.13.gate_in, s32[1,16,1,16]{3,2,1,0:T(1,128)} %ids_in.1, bf16[1,128,2048]{2,1,0:T(8,128)(2,1)} %q_in.1, bf16[1,128,2048]{2,1,0:T(8,128)(2,1)} %k_in.1, bf16[1,128,2048]{2,1,0:T(8,128)(2,1)} %v_in.1, ...), custom_call_target="tpu_custom_call" | custom-call | flops 5000000000 | bytes 5000000 | tf_op jit(solution)/shard_map/pallas_call | solution.py:451
  150.5 0.8 copy.11

commit v4 on v3

--- a/solution.py
+++ b/solution.py
@@ -127,7 +127,7 @@
             device_id={"mem": at_z(o)}, device_id_type=MESH,
         )
 
-    def scatter(a, src, dst, q=False):
+    def scatter(a, src, dst, q=False, held=0):
         copies = []
         for role, w in FAR_FIRST:
             o = offset(role, w)
@@ -137,8 +137,9 @@
                 dst.at[role, row * BLK : (row + 1) * BLK],
                 send_sem.at[a, role, w], recv_sem.at[a, role, w],
             )
+            copies.append(copy)
+        for copy in copies[: len(copies) - held]:
             copy.start()
-            copies.append(copy)
         return copies
 
     def w_copy(n, src, dst, peer):
@@ -183,20 +184,20 @@
         mkb[role, w * BLK : (w + 1) * BLK] = mk_old[:, columns]
         mvb[role, w * BLK : (w + 1) * BLK] = mv_old[:, columns]
 
-    for copy in own_q:
-        copy.wait()
-    for copy in q_copies:
-        copy.wait_recv()
     near, far = slice(0, KEYS), slice(KEYS, SEG)
     relays = [
         along_z(GAP, qb.at[0, near], qb.at[1, near], pass_send.at[0], pass_recv.at[0]),
         along_z(-GAP, qb.at[1, far], qb.at[0, far], pass_send.at[1], pass_recv.at[1]),
     ]
-    for copy in relays:
-        copy.start()
+    for relay, own_copy, role in zip(relays, own_q, ROLES, strict=True):
+        own_copy.wait()
+        for copy, (copy_role, _) in zip(q_copies, FAR_FIRST, strict=True):
+            if copy_role == role:
+                copy.wait_recv()
+        relay.start()
     mk_copies = scatter(2, mk_old, mkb)
     v_copies = scatter(3, v_in.at[0], vb)
-    mv_copies = scatter(4, mv_old, mvb)
+    mv_copies = scatter(4, mv_old, mvb, held=4)
 
     def block_at(role, u):
         return (z + u + (N - LEFT + head_shift(role))) & (N - 1)
@@ -314,10 +315,12 @@
 
     for copy in mk_copies:
         copy.wait_recv()
+    lse_copies = [
+        along_z(GAP, lse_out.at[0], lse_in.at[1], pass_send.at[2], pass_recv.at[2]),
+        along_z(-GAP, lse_out.at[1], lse_in.at[0], pass_send.at[3], pass_recv.at[3]),
+    ]
     for role in ROLES:
         lax.fori_loop(0, HALF, old_pair(role), 0)
-
-    for role in ROLES:
         for u in range(N):
             turned = jnp.transpose(stats[role, u * BLK : (u + 1) * BLK, :])
             for n in range(6):
@@ -325,11 +328,8 @@
         loc, seg, old = (lines[role, n] + log2(lines[role, n + 1]) for n in (0, 2, 4))
         lse_out[role, 0] = loc
         lse_out[role, 1] = join(seg, old)
-    lse_copies = [
-        along_z(GAP, lse_out.at[0], lse_in.at[1], pass_send.at[2], pass_recv.at[2]),
-        along_z(-GAP, lse_out.at[1], lse_in.at[0], pass_send.at[3], pass_recv.at[3]),
-    ]
-    for copy in lse_copies:
+        lse_copies[role].start()
+    for copy in mv_copies[-4:]:
         copy.start()
 
     for copy in own_v:

time: 153 us -> 152 us (level)
  no operation moved by 1% of the time
where the time goes in v4:
time: 152 us; the launch traced here: 151 us
  Pallas kernels  148 us (97%)
    pallas_call x1, Pallas kernels, local(): pl.pallas_call(functools.partial(kernel, dims), out_shape=pltpu.VMEM(quer...  148 us

profile of v4, /device:TPU:1, one launch (start us, length us, event | category | flops | bytes accessed | tf_op | source)
XLA Modules:
  0.0 150.6 jit_solution(8056698724496690897)
XLA Ops:
  1.3 148.5 %shard_map.91 = bf16[1,128,2048]{2,1,0:T(8,128)(2,1)S(1)} custom-call(s32[1]{0:T(128)S(6)} %copy.12.pointer_in, f32[1]{0:T(128)S(6)} %copy.13.gate_in, s32[1,16,1,16]{3,2,1,0:T(1,128)} %ids_in.1, bf16[1,128,2048]{2,1,0:T(8,128)(2,1)} %q_in.1, bf16[1,128,2048]{2,1,0:T(8,128)(2,1)} %k_in.1, bf16[1,128,2048]{2,1,0:T(8,128)(2,1)} %v_in.1, ...), custom_call_target="tpu_custom_call" | custom-call | flops 5000000000 | bytes 5000000 | tf_op jit(solution)/shard_map/pallas_call | solution.py:451
  149.8 0.8 copy.11
